TPU v7x, 32 devices: a whole 2x2x4 slice. The times are simulated.
32 devices in a mesh: groups: 2 (over y), fsdp: 4 (over z), dp: 2 (over x), pair: 2 (over core).
Axes of the slice: x: 2, y: 2, z: 4, core: 2. Of those that a mesh axis runs over, the one named last changes fastest.
Arguments:
- hidden_input: bfloat16 [4096, 8192], P(('groups', 'fsdp', 'dp', 'pair')), parts along dimension 0, may hold values from -6 to 6
- norm_gain_vector: float32 [8192], replicated, may hold values from 0.5 to 18, as said below
- value_matrix: bfloat16 [8192, 768], P('fsdp'), may hold values from -0.0625 to 0.0625
- adapter_down_map: bfloat16 [16384, 64], P(('groups', 'fsdp')), parts along dimension 0, may hold values from -0.0625 to 0.0625
- adapter_up_map: bfloat16 [128, 768], P('groups'), parts along dimension 0, may hold values from -5 to 5
- values_gradient: bfloat16 [4096, 768], P(('groups', 'fsdp', 'dp', 'pair')), parts along dimension 0, may hold values from -6 to 6
Outputs:
- grad_hidden: bfloat16 [4096, 8192], P(('groups', 'fsdp', 'dp', 'pair')), parts along dimension 0
- grad_down: float32 [16384, 64], P(('groups', 'fsdp')), parts along dimension 0
- grad_up: float32 [128, 768], P('groups'), parts along dimension 0
There are 2 independent parts, one for each index of `groups`. A program takes and returns all parts, laid end to end along the dimension named above; an argument that names none is the same for every part. Nothing has to cross between parts.
Inputs may be any that keep to these rules, and one draw needn't show every extreme that they name: `norm_gain_vector`: positive gains.
All inputs are finite; a program needn't handle non-finite values.
Results may differ from a plain program's by a relative error of at most 0.0085.
Values may be sent and summed in bfloat16 or wider, within the bound.
A program may use at most 64 MiB of HBM per device.

v0:
```python
import math
import jax
import jax.numpy as jnp
from jax import lax
from jax.sharding import PartitionSpec as P

MODEL_WIDTH = 8192
ADAPTER_RANK = 64
norm_eps = 1e-05
adapter_scale = 2.0


def contract_last(left, right):
    return lax.dot_general(
        left, right, (((1,), (1,)), ((), ())), preferred_element_type=jnp.float32
    )


def contract_leading(left, right):
    return lax.dot_general(
        left, right, (((0,), (0,)), ((), ())), preferred_element_type=jnp.float32
    )


def local(
    hidden_input, norm_gain_vector, value_matrix, adapter_down_map, adapter_up_map, values_gradient
):
    width = hidden_input.shape[1]
    stream = hidden_input.astype(jnp.float32)
    inv_rms = lax.rsqrt(jnp.mean(stream * stream, axis=1, keepdims=True) + norm_eps)
    normalized_input = (stream * inv_rms * norm_gain_vector).astype(jnp.bfloat16)
    upward_product = (
        adapter_scale
        * jnp.dot(values_gradient, adapter_up_map.T, preferred_element_type=jnp.float32)
    ).astype(jnp.bfloat16)
    every_values, every_upward = (
        lax.all_gather(values_gradient, "fsdp", axis=0, tiled=True),
        lax.all_gather(upward_product, "fsdp", axis=0, tiled=True),
    )
    columns = contract_last(every_values, value_matrix) + contract_last(
        every_upward, adapter_down_map
    )
    gradient_normalized = lax.all_to_all(
        columns.astype(jnp.bfloat16), "fsdp", split_axis=0, concat_axis=1, tiled=True
    )
    window = normalized_input
    latent_f = jnp.dot(
        window,
        lax.all_gather(adapter_down_map, "fsdp", axis=0, tiled=True),
        preferred_element_type=jnp.float32,
    )
    scaled = gradient_normalized.astype(jnp.float32) * norm_gain_vector
    grad_stream = inv_rms * scaled - stream * (inv_rms**3 / width) * jnp.sum(
        scaled * stream, axis=1, keepdims=True
    )
    latent_code = latent_f.astype(jnp.bfloat16)
    window = normalized_input
    down_shard = lax.psum_scatter(
        contract_leading(window, upward_product), "fsdp", scatter_dimension=0, tiled=True
    )
    up_portion = adapter_scale * contract_leading(latent_code, values_gradient)
    down_shard = lax.psum(down_shard, ("dp", "pair"))
    up_full = lax.psum(up_portion, ("fsdp", "dp", "pair"))
    total = lax.psum(jnp.sum(down_shard * down_shard), "fsdp") + jnp.sum(up_full * up_full)
    factor = jnp.minimum(1.0, 0.5 * math.sqrt(MODEL_WIDTH * ADAPTER_RANK) / jnp.sqrt(total))
    return (grad_stream.astype(jnp.bfloat16), factor * down_shard, factor * up_full)


def solution(mesh):
    return jax.shard_map(
        local,
        mesh=mesh,
        in_specs=(
            P(("groups", "fsdp", "dp", "pair"), None),
            P(),
            P("fsdp", None),
            P(("groups", "fsdp"), None),
            P("groups", None),
            P(("groups", "fsdp", "dp", "pair"), None),
        ),
        out_specs=(
            P(("groups", "fsdp", "dp", "pair"), None),
            P(("groups", "fsdp"), None),
            P("groups", None),
        ),
        check_vma=False,
    )
```

profile of v0, /device:TPU:0, one launch (start us, length us, event | category | flops | bytes accessed | tf_op | source)
XLA Modules:
  0.0 322.7 jit_solution(588120099054937987)
XLA Ops:
  7.2 0.0 copy-start
  7.2 0.0 reduce-scatter.2.cloned.1.call-start
  7.2 21.6 %all_gather.9 = bf16[512,768]{1,0:T(8,128)(2,1)S(1)} all-gather(bf16[128,768]{1,0:T(8,128)(2,1)} %param.11), channel_id=1, replica_groups=mesh['groups'=2,'fsdp'=4,'dp'=2,'pair'=2] {'fsdp'}, dimensions={0}, use_global_device_ids=true | all-gather | bytes 983040 | tf_op jit(solution)/shard_map/all_gather | solution.py:37
  28.9 1.2 fusion.7
  30.1 12.0 %all_gather.10 = bf16[512,64]{0,1:T(8,128)(2,1)S(1)} all-gather(bf16[128,64]{0,1:T(8,128)(2,1)S(1)} %fusion.7), channel_id=1, replica_groups=mesh['groups'=2,'fsdp'=4,'dp'=2,'pair'=2] {'fsdp'}, dimensions={0}, use_global_device_ids=true | all-gather | bytes 81920 | tf_op jit(solution)/shard_map/all_gather | solution.py:38
  42.0 0.0 copy-done
  42.1 0.0 copy-start.3
  42.1 1.8 fusion.13
  43.9 0.0 copy-done.3
  43.9 0.7 add_convert_fusion
  44.6 46.4 %all_to_all.13 = bf16[4,128,2048]{2,1,0:T(8,128)(2,1)S(1)} all-to-all(bf16[4,128,2048]{2,1,0:T(8,128)(2,1)S(1)} %bitcast.16), channel_id=1, replica_groups=mesh['groups'=2,'fsdp'=4,'dp'=2,'pair'=2] {'fsdp'}, dimensions={0} | all-to-all | bytes 4194304 | tf_op jit(solution)/shard_map/all_to_all | solution.py:43
  91.1 0.5 convert_bitcast_fusion
  91.6 0.0 copy-start.2
  91.6 0.0 copy-start.5
  91.6 0.5 copy.10
  92.1 0.0 copy-start.1
  92.1 1.9 copy-done.1
  94.0 0.0 copy-done.2
  94.0 0.0 copy-done.5
  94.0 1.2 fusion
  95.2 0.0 copy-start.4
  95.2 2.2 fusion.10
  97.4 0.0 reduce-scatter.2.cloned.1.call-update
  97.4 0.0 all-gather.2.cloned.1.call-start
  97.5 0.7 all-gather.2.cloned.1.call-update
  98.2 0.0 all-reduce.3.cloned.1.call-start
  98.2 42.3 %reduce-scatter.2.cloned.1.call-done = f32[2048,64]{0,1:T(8,128)} async-done(((f32[8192,64]{0,1:T(8,128)}), f32[2048,64]{0,1:T(8,128)}) %reduce-scatter.2.cloned.1.call-update) | async-done | bytes 524304 | tf_op jit(solution)/shard_map/reduce_scatter | solution.py:58
  140.5 0.0 all-reduce.3.cloned.1.call-update
  140.6 0.0 all-reduce.5.cloned.1.call-start
  140.6 28.9 %all-gather.2.cloned.1.call-done = bf16[8192,64]{0,1:T(8,128)(2,1)} async-done(((bf16[2048,64]{0,1:T(8,128)(2,1)}), bf16[8192,64]{0,1:T(8,128)(2,1)}) %all-gather.2.cloned.1.call-update) | async-done | bytes 1048592 | tf_op jit(solution)/shard_map/all_gather | solution.py:49
  169.5 0.0 copy-done.4
  169.5 3.5 %convolution_multiply_fusion = f32[64,768]{1,0:T(8,128)} fusion(bf16[128,768]{1,0:T(8,128)(2,1)S(1)} %copy-done.4, bf16[8192,64]{0,1:T(8,128)(2,1)} %all-gather.2.cloned.1.call-done, bf16[128,8192]{1,0:T(8,128)(2,1)} %param.6, f32[8192]{0:T(1024)S(1)} %copy-done.5, f32[128]{0:T(128)S(1)} %get-tuple-element.5), kind=kOutput, calls=%fused_computation.13 | convolution fusion | flops 151052288 | bytes 3572224 | tf_op jit(solution)/shard_map/dot_general | solution.py:20
  173.0 0.0 all-reduce.5.cloned.1.call-update
  173.1 5.3 %fusion.3 = bf16[128,8192]{1,0:T(8,128)(2,1)} fusion(bf16[128,8192]{1,0:T(8,128)(2,1)} %param.6, f32[128,8192]{1,0:T(8,128)} %bitcast.15, f32[128]{0:T(128)S(1)} %get-tuple-element.4, f32[128]{0:T(128)S(1)} %get-tuple-element.6, f32[8192]{0:T(1024)S(1)} %copy-done.5, f32[128]{0:T(128)S(1)} %get-tuple-element.5), kind=kLoop, calls=%fused_computation.7 | loop fusion | flops 7340032 | bytes 8422912 | tf_op jit(solution)/shard_map/convert_element_type | solution.py:66
  178.4 26.3 %all-reduce.3.cloned.1.call-done = f32[2048,64]{0,1:T(8,128)} async-done(((f32[2048,64]{0,1:T(8,128)}), f32[2048,64]{0,1:T(8,128)}) %all-reduce.3.cloned.1.call-update) | async-done | bytes 524304 | tf_op jit(solution)/shard_map/psum | solution.py:62
  204.7 1.8 multiply_reduce_fusion
  206.5 92.0 %all-reduce.5.cloned.1.call-done = f32[64,768]{1,0:T(8,128)} async-done(((f32[64,768]{1,0:T(8,128)}), f32[64,768]{1,0:T(8,128)}) %all-reduce.5.cloned.1.call-update) | async-done | bytes 196624 | tf_op jit(solution)/shard_map/psum | solution.py:63
  298.5 1.6 multiply_reduce_fusion.1
  300.1 11.2 %psum.22 = f32[]{:T(128)} all-reduce(f32[]{:T(128)} %multiply_reduce_fusion), channel_id=1, replica_groups=mesh['groups'=2,'fsdp'=4,'dp'=2,'pair'=2] {'fsdp'}, use_global_device_ids=true, to_apply=%region_5.0 | all-reduce | flops 1 | bytes 8 | tf_op jit(solution)/shard_map/psum | solution.py:64
  312.7 1.9 broadcast_multiply_fusion
  314.6 1.6 broadcast_multiply_fusion.1
  (1 shorter events, 0.0 us)
Async XLA Ops:
  7.2 34.9 %copy-start = (bf16[2048,768]{1,0:T(8,128)(2,1)S(1)}, bf16[2048,768]{1,0:T(8,128)(2,1)}, u32[]{:S(2)}) copy-start(bf16[2048,768]{1,0:T(8,128)(2,1)} %param.8) | copy-start | bytes 9437188
  7.2 133.4 %reduce-scatter.2.cloned.1.call-start = ((), (), s32[]{:S(2)}) async-start(), calls=%async_computation.2 | async-start | bytes 2621440 | tf_op jit(solution)/shard_map/reduce_scatter | solution.py:58
  42.1 1.8 copy-start.3
  91.6 2.5 copy-start.2
  91.6 2.4 copy-start.5
  92.1 1.9 copy-start.1
  95.2 74.3 %copy-start.4 = (bf16[128,768]{1,0:T(8,128)(2,1)S(1)}, bf16[128,768]{1,0:T(8,128)(2,1)}, u32[]{:S(2)}) copy-start(bf16[128,768]{1,0:T(8,128)(2,1)} %param.11) | copy-start | bytes 589828
  97.4 72.1 %all-gather.2.cloned.1.call-start = ((), (), s32[]{:S(2)}) async-start(), calls=%async_computation.4 | async-start | bytes 1310720 | tf_op jit(solution)/shard_map/all_gather | solution.py:49
  98.2 106.5 %all-reduce.3.cloned.1.call-start = ((), (), s32[]{:S(2)}) async-start(), calls=%async_computation.3 | async-start | bytes 1048576 | tf_op jit(solution)/shard_map/psum | solution.py:62
  140.6 157.9 %all-reduce.5.cloned.1.call-start = ((), (), s32[]{:S(2)}) async-start(), calls=%async_computation.5 | async-start | bytes 393216 | tf_op jit(solution)/shard_map/psum | solution.py:63
Sparse Core Ops, SparseCore 0:
  97.6 42.9 reduce-scatter.1
  142.2 27.2 all-gather.1
  172.0 32.6 all-reduce.2
  208.9 89.5 all-reduce.4
where the time goes:
time: 323 us
  waiting for transfers between devices  190 us (59%)
  blocking collectives  91.3 us (28%)
  between operations  15.2 us (5%)
  other arithmetic  13.9 us (4%)
  matrix products  9.43 us (3%)
    psum x1, waiting for transfers between devices, local(): up_full = lax.psum(up_portion, ('fsdp', 'dp', 'pair'))  92 us
    all_to_all x1, blocking collectives, local(): lax.all_to_all(columns.astype(jnp.bfloat16), 'fsdp', split_axis=0, concat...  46.4 us
    reduce_scatter x1, waiting for transfers between devices, local(): lax.psum_scatter(contract_leading(window, upward_product), 'fsdp', scatte...  42.3 us
    all_gather x1, waiting for transfers between devices, local(): lax.all_gather(adapter_down_map, 'fsdp', axis=0, tiled=True)  28.9 us
    psum x1, waiting for transfers between devices, local(): down_shard = lax.psum(down_shard, ('dp', 'pair'))  26.3 us
    all_gather x1, blocking collectives, local(): lax.all_gather(values_gradient, 'fsdp', axis=0, tiled=True)  21.6 us
    all_gather x1, blocking collectives, local(): lax.all_gather(upward_product, 'fsdp', axis=0, tiled=True)  12 us
    psum x1, blocking collectives, local(): lax.psum(jnp.sum(down_shard * down_shard), 'fsdp')  11.2 us
  transfers between devices with their start and end apart: 4, of which 4 were waited for; matrix products, arithmetic and copies ran while one was open for 3% of the time, Pallas kernels for 0%

commit v1 on v0

--- a/solution.py
+++ b/solution.py
@@ -8,6 +8,11 @@
 ADAPTER_RANK = 64
 norm_eps = 1e-05
 adapter_scale = 2.0
+
+
+def add_all(shard, axis):
+    shards = lax.all_gather(shard, axis)
+    return jnp.sum(shards, axis=0)
 
 
 def contract_last(left, right):
@@ -60,7 +65,7 @@
     )
     up_portion = adapter_scale * contract_leading(latent_code, values_gradient)
     down_shard = lax.psum(down_shard, ("dp", "pair"))
-    up_full = lax.psum(up_portion, ("fsdp", "dp", "pair"))
+    up_full = add_all(up_portion, ("fsdp", "dp", "pair"))
     total = lax.psum(jnp.sum(down_shard * down_shard), "fsdp") + jnp.sum(up_full * up_full)
     factor = jnp.minimum(1.0, 0.5 * math.sqrt(MODEL_WIDTH * ADAPTER_RANK) / jnp.sqrt(total))
     return (grad_stream.astype(jnp.bfloat16), factor * down_shard, factor * up_full)

time: 323 us -> 266 us (0.82)
  waiting for transfers between devices: 190 us -> 132 us
    psum x1 -> x0, waiting for transfers between devices: 92 us -> none  [local(): up_full = lax.psum(up_portion, ('fsdp', 'dp', 'pair'))]
    all_gather x0 -> x1, waiting for transfers between devices: none -> 28.6 us  [add_all(): shards = lax.all_gather(shard, axis)]
    psum x1, waiting for transfers between devices: 26.3 us -> 31.6 us  [local(): down_shard = lax.psum(down_shard, ('dp', 'pair'))]
  transfers between devices with their start and end apart: 4 -> 4, of which waited for: 4 -> 4; matrix products, arithmetic and copies ran while one was open for 3% -> 4% of each run, Pallas kernels for 0% -> 0%
where the time goes in v1:
time: 266 us
  waiting for transfers between devices  132 us (50%)
  blocking collectives  92.4 us (35%)
  between operations  15.2 us (6%)
  other arithmetic  14.1 us (5%)
  matrix products  9.44 us (4%)
    all_to_all x1, blocking collectives, local(): lax.all_to_all(columns.astype(jnp.bfloat16), 'fsdp', split_axis=0, concat...  46.4 us
    reduce_scatter x1, waiting for transfers between devices, local(): lax.psum_scatter(contract_leading(window, upward_product), 'fsdp', scatte...  42.3 us
    psum x1, waiting for transfers between devices, local(): down_shard = lax.psum(down_shard, ('dp', 'pair'))  31.6 us
    all_gather x1, waiting for transfers between devices, local(): lax.all_gather(adapter_down_map, 'fsdp', axis=0, tiled=True)  28.9 us
    all_gather x1, waiting for transfers between devices, add_all(): shards = lax.all_gather(shard, axis)  28.6 us
    all_gather x1, blocking collectives, local(): lax.all_gather(values_gradient, 'fsdp', axis=0, tiled=True)  21.6 us
    psum x1, blocking collectives, local(): lax.psum(jnp.sum(down_shard * down_shard), 'fsdp')  12.4 us
    all_gather x1, blocking collectives, local(): lax.all_gather(upward_product, 'fsdp', axis=0, tiled=True)  12 us
  transfers between devices with their start and end apart: 4, of which 4 were waited for; matrix products, arithmetic and copies ran while one was open for 4% of the time, Pallas kernels for 0%

profile of v1, /device:TPU:0, one launch (start us, length us, event | category | flops | bytes accessed | tf_op | source)
XLA Modules:
  0.0 266.0 jit_solution(15390486985316888922)
XLA Ops:
  7.2 0.0 copy-start
  7.2 0.0 reduce-scatter.2.cloned.1.call-start
  7.2 21.6 %all_gather.15 = bf16[512,768]{1,0:T(8,128)(2,1)S(1)} all-gather(bf16[128,768]{1,0:T(8,128)(2,1)} %param.11), channel_id=1, replica_groups=mesh['groups'=2,'fsdp'=4,'dp'=2,'pair'=2] {'fsdp'}, dimensions={0}, use_global_device_ids=true | all-gather | bytes 983040 | tf_op jit(solution)/shard_map/all_gather | solution.py:42
  28.9 1.2 fusion.7
  30.1 12.0 %all_gather.16 = bf16[512,64]{0,1:T(8,128)(2,1)S(1)} all-gather(bf16[128,64]{0,1:T(8,128)(2,1)S(1)} %fusion.7), channel_id=1, replica_groups=mesh['groups'=2,'fsdp'=4,'dp'=2,'pair'=2] {'fsdp'}, dimensions={0}, use_global_device_ids=true | all-gather | bytes 81920 | tf_op jit(solution)/shard_map/all_gather | solution.py:43
  42.0 0.0 copy-done
  42.1 0.0 copy-start.3
  42.1 1.8 fusion.13
  43.9 0.0 copy-done.3
  43.9 0.7 add_convert_fusion
  44.6 46.4 %all_to_all.13 = bf16[4,128,2048]{2,1,0:T(8,128)(2,1)S(1)} all-to-all(bf16[4,128,2048]{2,1,0:T(8,128)(2,1)S(1)} %bitcast.17), channel_id=1, replica_groups=mesh['groups'=2,'fsdp'=4,'dp'=2,'pair'=2] {'fsdp'}, dimensions={0} | all-to-all | bytes 4194304 | tf_op jit(solution)/shard_map/all_to_all | solution.py:48
  91.1 0.5 convert_bitcast_fusion
  91.6 0.0 copy-start.2
  91.6 0.0 copy-start.5
  91.6 0.5 copy.10
  92.1 0.0 copy-start.1
  92.1 1.9 copy-done.1
  94.0 0.0 copy-done.2
  94.0 0.0 copy-done.5
  94.0 1.2 fusion
  95.2 0.0 copy-start.4
  95.3 2.2 fusion.10
  97.4 0.0 reduce-scatter.2.cloned.1.call-update
  97.4 0.0 all-gather.4.cloned.1.call-start
  97.5 0.7 all-gather.4.cloned.1.call-update
  98.2 0.0 all-reduce.2.cloned.1.call-start
  98.2 42.3 %reduce-scatter.2.cloned.1.call-done = f32[2048,64]{0,1:T(8,128)} async-done(((f32[8192,64]{0,1:T(8,128)}), f32[2048,64]{0,1:T(8,128)}) %reduce-scatter.2.cloned.1.call-update) | async-done | bytes 524304 | tf_op jit(solution)/shard_map/reduce_scatter | solution.py:63
  140.6 0.0 all-reduce.2.cloned.1.call-update
  140.6 0.0 all-gather.6.cloned.1.call-start
  140.6 28.9 %all-gather.4.cloned.1.call-done = bf16[8192,64]{0,1:T(8,128)(2,1)} async-done(((bf16[2048,64]{0,1:T(8,128)(2,1)}), bf16[8192,64]{0,1:T(8,128)(2,1)}) %all-gather.4.cloned.1.call-update) | async-done | bytes 1048592 | tf_op jit(solution)/shard_map/all_gather | solution.py:54
  169.5 0.0 copy-done.4
  169.5 3.5 %convolution_multiply_fusion = f32[64,768]{1,0:T(8,128)} fusion(bf16[128,768]{1,0:T(8,128)(2,1)S(1)} %copy-done.4, bf16[8192,64]{0,1:T(8,128)(2,1)} %all-gather.4.cloned.1.call-done, bf16[128,8192]{1,0:T(8,128)(2,1)} %param.6, f32[8192]{0:T(1024)S(1)} %copy-done.5, f32[128]{0:T(128)S(1)} %get-tuple-element.5), kind=kOutput, calls=%fused_computation.13 | convolution fusion | flops 151052288 | bytes 3572224 | tf_op jit(solution)/shard_map/dot_general | solution.py:25
  173.0 0.0 all-gather.6.cloned.1.call-update
  173.1 31.6 %all-reduce.2.cloned.1.call-done = f32[2048,64]{0,1:T(8,128)} async-done(((f32[2048,64]{0,1:T(8,128)}), f32[2048,64]{0,1:T(8,128)}) %all-reduce.2.cloned.1.call-update) | async-done | bytes 524304 | tf_op jit(solution)/shard_map/psum | solution.py:67
  204.7 1.8 multiply_reduce_fusion
  206.5 5.3 %fusion.3 = bf16[128,8192]{1,0:T(8,128)(2,1)} fusion(bf16[128,8192]{1,0:T(8,128)(2,1)} %param.6, f32[128,8192]{1,0:T(8,128)} %bitcast.16, f32[128]{0:T(128)S(1)} %get-tuple-element.4, f32[128]{0:T(128)S(1)} %get-tuple-element.6, f32[8192]{0:T(1024)S(1)} %copy-done.5, f32[128]{0:T(128)S(1)} %get-tuple-element.5), kind=kLoop, calls=%fused_computation.7 | loop fusion | flops 7340032 | bytes 8422912 | tf_op jit(solution)/shard_map/convert_element_type | solution.py:71
  211.8 12.4 %psum.15 = f32[]{:T(128)} all-reduce(f32[]{:T(128)} %multiply_reduce_fusion), channel_id=1, replica_groups=mesh['groups'=2,'fsdp'=4,'dp'=2,'pair'=2] {'fsdp'}, use_global_device_ids=true, to_apply=%region_5.0 | all-reduce | flops 1 | bytes 8 | tf_op jit(solution)/shard_map/psum | solution.py:69
  224.2 28.6 %all-gather.6.cloned.1.call-done = f32[1024,768]{1,0:T(8,128)} async-done(((f32[64,768]{1,0:T(8,128)}), f32[1024,768]{1,0:T(8,128)}) %all-gather.6.cloned.1.call-update) | async-done | bytes 3145744 | tf_op jit(solution)/shard_map/all_gather | solution.py:14
  252.8 2.1 reduce_sum.48
  254.9 0.6 multiply_reduce_fusion.1
  256.9 0.7 broadcast_multiply_fusion.1
  257.6 1.9 broadcast_multiply_fusion
  (1 shorter events, 0.0 us)
Async XLA Ops:
  7.2 34.9 %copy-start = (bf16[2048,768]{1,0:T(8,128)(2,1)S(1)}, bf16[2048,768]{1,0:T(8,128)(2,1)}, u32[]{:S(2)}) copy-start(bf16[2048,768]{1,0:T(8,128)(2,1)} %param.8) | copy-start | bytes 9437188
  7.2 133.4 %reduce-scatter.2.cloned.1.call-start = ((), (), s32[]{:S(2)}) async-start(), calls=%async_computation.2 | async-start | bytes 2621440 | tf_op jit(solution)/shard_map/reduce_scatter | solution.py:63
  42.1 1.8 copy-start.3
  91.6 2.5 copy-start.2
  91.6 2.4 copy-start.5
  92.1 1.9 copy-start.1
  95.2 74.3 %copy-start.4 = (bf16[128,768]{1,0:T(8,128)(2,1)S(1)}, bf16[128,768]{1,0:T(8,128)(2,1)}, u32[]{:S(2)}) copy-start(bf16[128,768]{1,0:T(8,128)(2,1)} %param.11) | copy-start | bytes 589828
  97.4 72.1 %all-gather.4.cloned.1.call-start = ((), (), s32[]{:S(2)}) async-start(), calls=%async_computation.4 | async-start | bytes 1310720 | tf_op jit(solution)/shard_map/all_gather | solution.py:54
  98.2 106.5 %all-reduce.2.cloned.1.call-start = ((), (), s32[]{:S(2)}) async-start(), calls=%async_computation.3 | async-start | bytes 1048576 | tf_op jit(solution)/shard_map/psum | solution.py:67
  140.6 112.2 %all-gather.6.cloned.1.call-start = ((), (), s32[]{:S(2)}) async-start(), calls=%async_computation.5 | async-start | bytes 3342336 | tf_op jit(solution)/shard_map/all_gather | solution.py:14
Sparse Core Ops, SparseCore 0:
  97.6 42.9 reduce-scatter.1
  142.2 27.2 all-gather.3
  172.0 32.6 all-reduce.1
  207.7 45.1 all-gather.5
